TPU v7x, 32 devices: a whole 2x2x4 slice. The times are simulated.
32 devices in a mesh: group: 2 (over x), row: 16 (over z, y, core).
Axes of the slice: x: 2, y: 2, z: 4, core: 2. Of those that a mesh axis runs over, the one named last changes fastest.
Arguments:
- gram_tiles: bfloat16 [4, 16384, 16384], P('group', 'row'), parts along dimension 0, as said below
- weight_panels: bfloat16 [4, 16384, 128], P('group', 'row'), parts along dimension 0, may hold values from -6 to 6
Outputs:
- merged: float32 [32768, 128], P(('group', 'row')), parts along dimension 0
- residual: float32 [32768, 128], P(('group', 'row')), parts along dimension 0
There are 2 independent parts, one for each index of `group`. A program takes and returns all parts, laid end to end along the dimension named above; each array names one. Nothing has to cross between parts.
Inputs may be any that keep to these rules, and one draw needn't show every extreme that they name: `gram_tiles`: each of the 2 Grams is exactly symmetric.
All inputs are finite; a program needn't handle non-finite values.
Results may differ from a plain program's by a relative error of at most 0.0003.
Values may be sent and summed in bfloat16 or wider, within the bound.
No kernel may reach another device: no remote copies, remote signals or barrier semaphores. Data moves between devices by JAX's collectives and lax.ppermute only.
A program may use at most 320 MiB of HBM per device.

v0:
```python
import jax
import jax.numpy as jnp
from jax import lax
from jax.sharding import PartitionSpec as P

ITERS = 2


def on_device(gram_tiles, weight_panels):
    tile_rows = gram_tiles.shape[1]
    full_width = gram_tiles.shape[2]
    panel_cols = weight_panels.shape[2]
    first_row = lax.axis_index("row") * tile_rows
    row_ids = lax.broadcasted_iota(jnp.int32, (tile_rows, full_width), 0) + first_row
    col_ids = lax.broadcasted_iota(jnp.int32, (tile_rows, full_width), 1)
    operator_rows = jnp.sum(gram_tiles.astype(jnp.float32), axis=0) + jnp.where(
        row_ids == col_ids, 1.0, 0.0
    )
    right = jnp.einsum(
        "mrc,mck->rk",
        gram_tiles,
        lax.all_gather(weight_panels, "row", axis=1, tiled=True),
        preferred_element_type=jnp.float32,
    )

    def squares(vector_in):
        return lax.psum(jnp.sum(vector_in * vector_in, axis=0), "row")

    merged = jnp.zeros((tile_rows, panel_cols), jnp.float32)
    cg_residual = right
    direction = right
    norm_now = squares(cg_residual)
    for iteration in range(ITERS):
        applied = jnp.dot(
            operator_rows,
            lax.all_gather(direction, "row", axis=0, tiled=True),
            precision=lax.Precision.HIGHEST,
            preferred_element_type=jnp.float32,
        )
        curvature = lax.psum(jnp.sum(direction * applied, axis=0), "row")
        step_size = norm_now / curvature
        merged = merged + step_size * direction
        cg_residual = cg_residual - step_size * applied
        norm_next = squares(cg_residual)
        direction = cg_residual + norm_next / norm_now * direction
        norm_now = norm_next
    return (merged, cg_residual)


def solution(mesh):
    in_specs = (P("group", "row", None), P("group", "row", None))
    out_specs = (P(("group", "row"), None), P(("group", "row"), None))
    return jax.shard_map(
        on_device, mesh=mesh, in_specs=in_specs, out_specs=out_specs, check_vma=False
    )
```

profile of v0, /device:TPU:0, one launch (start us, length us, event | category | flops | bytes accessed | tf_op | source)
XLA Modules:
  0.0 489.9 jit_solution(12920156381895548868)
XLA Ops:
  7.2 0.0 all-gather.4.cloned.1.call-start
  7.2 0.7 all-gather.4.cloned.1.call-update
  7.9 0.0 all-gather.6.cloned.1.call-start
  7.9 79.9 %all-gather.4.cloned.1.call-done = bf16[2,16384,128]{2,1,0:T(8,128)(2,1)} async-done(((bf16[2,1024,128]{2,1,0:T(8,128)(2,1)}), bf16[2,16384,128]{2,1,0:T(8,128)(2,1)}) %all-gather.4.cloned.1.call-update) | async-done | bytes 8388624 | tf_op jit(solution)/shard_map/all_gather | solution.py:22
  87.9 29.5 %convolution_bitcast_fusion = f32[1024,128]{1,0:T(8,128)} fusion(bf16[2,1024,16384]{2,1,0:T(8,128)(2,1)} %param.2, bf16[2,16384,128]{2,1,0:T(8,128)(2,1)} %all-gather.4.cloned.1.call-done), kind=kOutput, calls=%fused_computation.11 | convolution fusion | flops 8589934592 | bytes 76021760 | tf_op jit(solution)/shard_map/mrc,mck->rk/dot_general | solution.py:19
  117.3 0.0 all-gather.6.cloned.1.call-update
  117.4 0.2 all-gather.8.cloned.1.call-start
  117.6 0.0 copy-start
  117.6 45.0 %convert_reduce_fusion = f32[1024,16384]{1,0:T(8,128)} fusion(bf16[2,1024,16384]{2,1,0:T(8,128)(2,1)} %param.2), kind=kLoop, calls=%fused_computation | loop fusion | flops 50331648 | bytes 134217728 | tf_op jit(solution)/shard_map/reduce_sum | solution.py:16
  162.6 28.1 %all-gather.6.cloned.1.call-done = f32[16384,128]{1,0:T(8,128)} async-done(((f32[1024,128]{1,0:T(8,128)}), f32[16384,128]{1,0:T(8,128)}) %all-gather.6.cloned.1.call-update) | async-done | bytes 8388624 | tf_op jit(solution)/shard_map/all_gather | solution.py:36
  190.7 0.0 copy-done
  190.7 63.3 %multiply_reduce_fusion.2 = (f32[128]{0:T(128)S(1)}, f32[128]{0:T(128)S(1)}, f32[1024,128]{1,0:T(8,128)S(1)}) fusion(f32[1024,128]{1,0:T(8,128)S(1)} %copy-done, f32[16384,128]{1,0:T(8,128)} %all-gather.6.cloned.1.call-done, f32[1024,16384]{1,0:T(8,128)} %convert_reduce_fusion, s32[1024]{0:T(1024)S(1)} %iota_add_fusion), kind=kOutput, calls=%fused_computation.18 | convolution fusion | flops 25820659712 | bytes 76551168 | tf_op jit(solution)/shard_map/dot_general | solution.py:34
  253.9 31.0 %all-reduce = (f32[128]{0:T(128)S(1)}, f32[128]{0:T(128)S(1)}) all-reduce(f32[128]{0:T(128)S(1)} %get-tuple-element.3, f32[128]{0:T(128)S(1)} %get-tuple-element.2), channel_id=1, replica_groups=mesh['group'=2,'row'=16] {'row'}, use_global_device_ids=true, to_apply=%region_1.2 | all-reduce | flops 256 | bytes 2048 | tf_op jit(solution)/shard_map/psum | solution.py:27
  284.9 0.2 multiply_reduce_fusion.1
  285.1 29.7 %psum.30 = f32[128]{0:T(128)S(1)} all-reduce(f32[128]{0:T(128)S(1)} %multiply_reduce_fusion.1), channel_id=1, replica_groups=mesh['group'=2,'row'=16] {'row'}, use_global_device_ids=true, to_apply=%region_6.7 | all-reduce | flops 128 | bytes 1024 | tf_op jit(solution)/shard_map/psum | solution.py:27
  314.8 0.9 multiply_add_fusion.1
  315.6 0.0 copy-start.1
  315.6 0.0 all-gather.8.cloned.1.call-update
  315.7 72.2 %all-gather.8.cloned.1.call-done = f32[16384,128]{1,0:T(8,128)} async-done(((f32[1024,128]{1,0:T(8,128)}), f32[16384,128]{1,0:T(8,128)}) %all-gather.8.cloned.1.call-update) | async-done | bytes 8388624 | tf_op jit(solution)/shard_map/all_gather | solution.py:36
  387.9 63.4 %multiply_reduce_fusion = (f32[128]{0:T(128)S(1)}, f32[1024,128]{1,0:T(8,128)S(1)}) fusion(f32[1024,128]{1,0:T(8,128)} %multiply_add_fusion.1, f32[16384,128]{1,0:T(8,128)} %all-gather.8.cloned.1.call-done, f32[1024,16384]{1,0:T(8,128)} %convert_reduce_fusion, s32[1024]{0:T(1024)S(1)} %iota_add_fusion), kind=kOutput, calls=%fused_computation.14 | convolution fusion | flops 25820397568 | bytes 76550656 | tf_op jit(solution)/shard_map/dot_general | solution.py:34
  451.3 31.0 %psum.31 = f32[128]{0:T(128)S(1)} all-reduce(f32[128]{0:T(128)S(1)} %get-tuple-element.9), channel_id=1, replica_groups=mesh['group'=2,'row'=16] {'row'}, use_global_device_ids=true, to_apply=%region_8.9 | all-reduce | flops 128 | bytes 1024 | tf_op jit(solution)/shard_map/psum | solution.py:40
  482.3 0.0 copy-done.1
  482.3 1.1 multiply_subtract_fusion
  (4 shorter events, 0.0 us)
Async XLA Ops:
  7.2 80.7 %all-gather.4.cloned.1.call-start = ((), (), s32[]{:S(2)}) async-start(), calls=%async_computation | async-start | bytes 8912896 | tf_op jit(solution)/shard_map/all_gather | solution.py:22
  7.9 182.8 %all-gather.6.cloned.1.call-start = ((), (), s32[]{:S(2)}) async-start(), calls=%async_computation.1 | async-start | bytes 8912896 | tf_op jit(solution)/shard_map/all_gather | solution.py:36
  117.4 270.5 %all-gather.8.cloned.1.call-start = ((), (), s32[]{:S(2)}) async-start(), calls=%async_computation.2 | async-start | bytes 8912896 | tf_op jit(solution)/shard_map/all_gather | solution.py:36
  117.6 73.0 %copy-start = (f32[1024,128]{1,0:T(8,128)S(1)}, f32[1024,128]{1,0:T(8,128)}, u32[]{:S(2)}) copy-start(f32[1024,128]{1,0:T(8,128)} %convolution_bitcast_fusion) | copy-start | bytes 1572868
  315.6 166.6 %copy-start.1 = (f32[1024,128]{1,0:T(8,128)S(1)}, f32[1024,128]{1,0:T(8,128)}, u32[]{:S(2)}) copy-start(f32[1024,128]{1,0:T(8,128)} %multiply_add_fusion.1) | copy-start | bytes 1572868
Sparse Core Ops, SparseCore 0:
  10.2 77.6 all-gather.3
  117.5 73.1 all-gather.5
  315.8 72.0 all-gather.7
where the time goes:
time: 491 us; the launch traced here: 490 us
  waiting for transfers between devices  181 us (37%)
  matrix products  156 us (32%)
  blocking collectives  91.7 us (19%)
  other arithmetic  47.2 us (10%)
  between operations  13.8 us (3%)
    dot_general x2, matrix products, on_device(): jnp.dot(operator_rows, lax.all_gather(direction, 'row', axis=0, tiled=Tru...  127 us
    all_gather x2, waiting for transfers between devices, on_device(): lax.all_gather(direction, 'row', axis=0, tiled=True)  100 us
    all_gather x1, waiting for transfers between devices, on_device(): lax.all_gather(weight_panels, 'row', axis=1, tiled=True)  79.9 us
    psum x2, blocking collectives, squares(): return lax.psum(jnp.sum(vector_in * vector_in, axis=0), 'row')  60.7 us
    reduce_sum x1, other arithmetic, on_device(): jnp.sum(gram_tiles.astype(jnp.float32), axis=0)  45 us
    psum x1, blocking collectives, on_device(): curvature = lax.psum(jnp.sum(direction * applied, axis=0), 'row')  31 us
    dot_general x1, matrix products, on_device(): jnp.einsum('mrc,mck->rk', gram_tiles, lax.all_gather(weight_panels, 'row'...  29.5 us
  transfers between devices with their start and end apart: 3, of which 3 were waited for; matrix products, arithmetic and copies ran while one was open for 9% of the time, Pallas kernels for 0%

commit v1 on v0

v1 whole, which is shorter than its diff:
```python
import functools
import jax
import jax.numpy as jnp
from jax import lax
from jax.experimental import pallas as pl
from jax.experimental.pallas import tpu as pltpu
from jax.sharding import PartitionSpec as P

EXTRA = 16


def split_pair(x):
    hi = x.astype(jnp.bfloat16)
    return hi, (x - hi.astype(jnp.float32)).astype(jnp.bfloat16)


SPAN, LOWEST = 29.75, -14.0


def coded_block(x):
    top = jnp.maximum(jnp.max(jnp.abs(x), axis=0, keepdims=True), 1e-30)
    exponent = jnp.floor(jnp.log2(top)) - 4.0
    factor = jnp.ceil(top * jnp.exp2(-exponent) * (512.0 / SPAN)) * (1.0 / 512.0)
    size = jnp.abs(x) / (factor * jnp.exp2(exponent))
    code = jnp.exp2(size + LOWEST)
    row = lax.broadcasted_iota(jnp.int32, (EXTRA, x.shape[1]), 0)
    return jnp.where(x < 0, -code, code), jnp.where(row == 0, exponent, factor)


def decoded_block(code, extra):
    binade = extra[1:2] * jnp.exp2(extra[0:1])
    size = (jnp.log2(jnp.abs(code)) - LOWEST) * binade
    return jnp.where(code < 0, -size, size)


def product_kernel(cfg, ids_ref, gram_ref, *refs):
    blocks, own, panels, has_total, tail = cfg
    refs = list(refs)
    x_refs = [refs.pop(0) for _ in range(blocks)]
    total_ref = refs.pop(0) if has_total else None
    base_ref = refs.pop(0) if tail == "moments" else None
    out_ref = refs.pop(0)
    more_ref = refs.pop(0) if tail else None
    acc, held = refs
    block, piece = pl.program_id(0), pl.program_id(1)
    models, rows, depth = gram_ref.shape
    cols = out_ref.shape[1]

    @pl.when((block == 0) & (piece == 0))
    def _():
        if has_total:
            acc[:, :cols] = total_ref[...]
        else:
            acc[:, :cols] = jnp.zeros((rows, cols), jnp.float32)
        if not panels:
            acc[:, cols:] = jnp.zeros((rows, cols), jnp.float32)

    for i in range(blocks):
        @pl.when((block == i) & (piece == 0))
        def _(i=i):
            if panels:
                held[...] = x_refs[i][...]
                return
            x = x_refs[i][:rows, :]
            if own and i == 0:
                acc[:, :cols] += x
            else:
                x = decoded_block(x, x_refs[i][rows:, :])
            hi, lo = split_pair(x)
            held[:, :cols] = hi
            held[:, cols:] = lo

    at = pl.ds(pl.multiple_of(piece * depth, depth), depth)
    dot = functools.partial(jnp.dot, preferred_element_type=jnp.float32)
    if panels:
        acc[...] += sum(dot(gram_ref[m], held[m, at, :]) for m in range(models))
    else:
        acc[...] += sum(dot(gram_ref[m], held[at, :]) for m in range(models))

    @pl.when((block == blocks - 1) & (piece == pl.num_programs(1) - 1))
    def _():
        result = acc[...] if panels else acc[:, :cols] + acc[:, cols:]
        out_ref[...] = result
        if tail == "send":
            more_ref[:rows, :], more_ref[rows:, :] = coded_block(result)
        if tail == "moments":
            one, two = base_ref[0], base_ref[1]
            pairs = ((one, one), (one, two), (two, two), (two, result))
            sums = [jnp.sum(a * b, axis=0, keepdims=True) for a, b in pairs]
            more_ref[...] = jnp.concatenate(sums + [jnp.zeros((8 - len(sums), cols), jnp.float32)], axis=0)


def product(gram, ids, xs, total=None, *, own=False, panels=False, tail=None, base=None):
    models, rows, _ = gram.shape
    cols = xs[0].shape[-1]
    blocks = len(xs)
    depth = min(1024, rows)
    pieces = rows // depth
    cfg = (blocks, own, panels, total is not None, tail)
    whole = lambda a: pl.BlockSpec(a.shape, lambda b, k, ids: (0,) * a.ndim)
    inputs = list(xs)
    if total is not None:
        inputs.append(total)
    if tail == "moments":
        inputs.append(base)
    outs = [jax.ShapeDtypeStruct((rows, cols), jnp.float32)]
    if tail == "send":
        outs.append(jax.ShapeDtypeStruct((rows + EXTRA, cols), jnp.float32))
    if tail == "moments":
        outs.append(jax.ShapeDtypeStruct((8, cols), jnp.float32))
    width = cols if panels else 2 * cols
    held = (models, rows, cols) if panels else (rows, 2 * cols)
    result = pl.pallas_call(
        functools.partial(product_kernel, cfg),
        out_shape=outs,
        grid_spec=pltpu.PrefetchScalarGridSpec(
            num_scalar_prefetch=1,
            grid=(blocks, pieces),
            in_specs=[
                pl.BlockSpec((models, rows, depth), lambda b, k, ids: (0, 0, ids[b] * pieces + k))
            ] + [whole(a) for a in inputs],
            out_specs=[whole(o) for o in outs],
            scratch_shapes=[
                pltpu.VMEM((rows, width), jnp.float32),
                pltpu.VMEM(held, jnp.bfloat16),
            ],
        ),
        compiler_params=pltpu.CompilerParams(
            dimension_semantics=("arbitrary", "arbitrary"), vmem_limit_bytes=40 * 1024 * 1024
        ),
        cost_estimate=pl.CostEstimate(
            flops=2 * models * rows * rows * blocks * width,
            bytes_accessed=2 * models * rows * rows * blocks,
            transcendentals=0,
        ),
    )(ids, gram, *inputs)
    return result if tail else result[0]


def on_device(devices, gram, panel_rows):
    models, rows, _ = gram.shape
    cols = panel_rows.shape[2]
    chips = devices // 2
    order = list(range(0, chips, 2)) + list(range(chips - 1, 0, -2))
    place_of = [order.index(c) for c in range(chips)]

    def ring(step):
        return [
            (2 * c + core, 2 * order[(j + step) % chips] + core)
            for j, c in enumerate(order) for core in range(2)
        ]

    onward, back = ring(1), ring(-1)
    pair = [(i, i ^ 1) for i in range(devices)]
    send = lambda x, perm: lax.ppermute(x, "row", perm)
    me = lax.axis_index("row")
    core = lax.rem(me, 2)
    chip = me // 2
    place = jnp.where(lax.rem(chip, 2) == 0, chip // 2, chips - 1 - chip // 2)

    def device_at(place):
        place = lax.rem(place + 2 * chips, chips)
        return 2 * jnp.where(place < chips // 2, 2 * place, 2 * (chips - 1 - place) + 1)

    def ids_of(places):
        base = jnp.stack([device_at(p) for p in places])
        return jnp.concatenate([base + core, base + 1 - core]).astype(jnp.int32)

    ids_own = jnp.stack([me, me + 1 - 2 * core]).astype(jnp.int32)

    def gathered(own_block, sent, axis, cut, widen, *, own, panels, tail, base=None):
        call = functools.partial(product, gram, panels=panels)
        beside = send(sent, pair)
        ahead, behind = send(sent, onward), send(sent, back)
        total = call(ids_own, [own_block, widen(beside)], own=own)
        for step in range(1, chips // 2):
            ahead, behind, total = lax.optimization_barrier((ahead, behind, total))
            across = [send(ahead, pair), send(behind, pair)]
            blocks = [widen(x) for x in [ahead, behind] + across]
            if step + 1 < chips // 2:
                ahead, behind = send(ahead, onward), send(behind, back)
            else:
                first = send(lax.slice_in_dim(ahead, 0, cut, axis=axis), onward)
                second = send(lax.slice_in_dim(behind, cut, None, axis=axis), back)
            total = call(ids_of([place - step, place + step]), blocks, total)
        first, second, total = lax.optimization_barrier((first, second, total))
        far = jnp.concatenate([first, second], axis=axis)
        return call(
            ids_of([place + chips // 2]), [widen(far), widen(send(far, pair))], total, tail=tail, base=base
        )

    def vector_stage(x, scaled, **kw):
        return gathered(
            x, scaled.astype(jnp.float16), 0, rows // 2, lambda y: y.astype(jnp.float32),
            own=True, panels=False, **kw
        )

    right, scaled = gathered(
        panel_rows, panel_rows, 1, rows // 2, lambda y: y, own=False, panels=True, tail="send"
    )
    first, scaled = vector_stage(right, scaled, tail="send")
    second, sums = vector_stage(first, scaled, tail="moments", base=jnp.stack([right, first]))

    if devices & (devices - 1):
        sums = lax.psum(sums, "row")
    else:
        bit = 1
        while bit < devices:
            masks = [1, 2, 3] if bit == 1 and devices > 2 else [bit]
            sums = sum([send(sums, [(i, i ^ m) for i in range(devices)]) for m in masks], sums)
            bit *= len(masks) + 1

    norm_now, along, square, cube = (sums[i : i + 1] for i in range(4))
    step_one = norm_now / along
    norm_next = norm_now - 2.0 * step_one * along + step_one * step_one * square
    ratio = norm_next / norm_now
    lead = 1.0 + ratio
    curvature = lead * lead * along - 2.0 * lead * step_one * square + step_one * step_one * cube
    step_two = norm_next / curvature
    direction = lead * right - step_one * first
    merged = step_one * right + step_two * direction
    residual = right - step_one * first - step_two * (lead * first - step_one * second)
    return merged, residual


def solution(mesh):
    in_specs = (P("group", "row", None), P("group", "row", None))
    out_specs = (P(("group", "row"), None), P(("group", "row"), None))
    return jax.shard_map(
        functools.partial(on_device, mesh.shape["row"]),
        mesh=mesh, in_specs=in_specs, out_specs=out_specs, check_vma=False,
    )
```

time: 491 us -> 193 us (0.39)
  waiting for transfers between devices: 181 us -> 24.9 us
  matrix products: 156 us -> 0 us
  Pallas kernels: 0 us -> 120 us
  blocking collectives: 91.7 us -> 0 us
  other arithmetic: 47.2 us -> 3.09 us
  starting transfers between devices: 0.3 us -> 37.3 us
  between operations: 13.8 us -> 1.38 us
  local copies, waits for them, and re-layouts: 0.01 us -> 5.09 us
    all_gather x3 -> x0, waiting for transfers between devices: 180 us -> none  [the longest x2 100 us: on_device(): lax.all_gather(direction, 'row', axis=0, tiled=True)]
    dot_general x3 -> x0, matrix products: 156 us -> none  [the longest x2 127 us: on_device(): jnp.dot(operator_rows, lax.all_gather(direction, 'row', axis=0, tiled=Tru...]
    pallas_call x0 -> x15, Pallas kernels: none -> 120 us  [product(): pl.pallas_call(functools.partial(product_kernel, cfg), out_shape=outs, gr...]
    psum x3 -> x0, blocking collectives: 91.7 us -> none  [the longest x2 60.7 us: squares(): return lax.psum(jnp.sum(vector_in * vector_in, axis=0), 'row')]
    reduce_sum x2 -> x0, other arithmetic: 45.1 us -> none  [the longest x1 45 us: on_device(): jnp.sum(gram_tiles.astype(jnp.float32), axis=0)]
    ppermute x0 -> x53, starting transfers between devices: none -> 37.3 us  [on_device(): send = lambda x, perm: lax.ppermute(x, 'row', perm)]
    ppermute x0 -> x53, waiting for transfers between devices: none -> 24.9 us  [on_device(): send = lambda x, perm: lax.ppermute(x, 'row', perm)]
  transfers between devices with their start and end apart: 3 -> 53, of which waited for: 3 -> 16; matrix products, arithmetic and copies ran while one was open for 9% -> 1% of each run, Pallas kernels for 0% -> 53%
where the time goes in v1:
time: 193 us; the launch traced here: 192 us
  Pallas kernels  120 us (62%)
  starting transfers between devices  37.3 us (19%)
  waiting for transfers between devices  24.9 us (13%)
  local copies, waits for them, and re-layouts  5.09 us (3%)
  other arithmetic  3.09 us (2%)
    pallas_call x15, Pallas kernels, product(): pl.pallas_call(functools.partial(product_kernel, cfg), out_shape=outs, gr...  120 us
    ppermute x53, starting transfers between devices, on_device(): send = lambda x, perm: lax.ppermute(x, 'row', perm)  37.3 us
    ppermute x53, waiting for transfers between devices, on_device(): send = lambda x, perm: lax.ppermute(x, 'row', perm)  24.9 us
    unnamed x17, local copies, waits for them, and re-layouts  4.8 us
  transfers between devices with their start and end apart: 53, of which 16 were waited for; matrix products, arithmetic and copies ran while one was open for 1% of the time, Pallas kernels for 53%

profile of v1, /device:TPU:0, one launch (start us, length us, event | category | flops | bytes accessed | tf_op | source)
XLA Modules:
  0.0 192.1 jit_solution(5398168012622009927)
XLA Ops:
  0.6 0.5 collective-permute-start.2
  1.1 2.6 %collective-permute-start.1 = (bf16[2,1024,128]{2,1,0:T(8,128)(2,1)}, bf16[2,1024,128]{2,1,0:T(8,128)(2,1)S(1)}, u32[]{:S(2)}, u32[]{:S(2)}) collective-permute-start(bf16[2,1024,128]{2,1,0:T(8,128)(2,1)} %refs_0_.1), channel_id=1, source_target_pairs={{0,2},{1,3},{4,0},{5,1},{8,4},{9,5},{12,8},{13,9},{14,12},{15,13},... | collective-permute-start | bytes 1572872 | tf_op jit(solution)/shard_map/ppermute | solution.py:155
  4.0 1.0 copy-done.2
  5.0 5.4 %shard_map.41.refs_4_ = f32[1024,128]{1,0:T(8,128)S(1)} custom-call(s32[2]{0:T(128)S(1)} %pad_add_fusion.1.ids_ref, bf16[2,1024,16384]{2,1,0:T(8,128)(2,1)} %gram_ref.29, bf16[2,1024,128]{2,1,0:T(8,128)(2,1)S(1)} %copy-done.2, bf16[2,1024,128]{2,1,0:T(8,128)(2,1)S(1)} %collective-permute-done.2.refs_1_), custom_call_target="tpu_custom_call" | custom-call | flops 1073741824 | bytes 8388608 | tf_op jit(solution)/shard_map/pallas_call | solution.py:113
  10.4 6.1 %collective-permute-done.1.refs_1_ = bf16[2,1024,128]{2,1,0:T(8,128)(2,1)S(1)} collective-permute-done((bf16[2,1024,128]{2,1,0:T(8,128)(2,1)}, bf16[2,1024,128]{2,1,0:T(8,128)(2,1)S(1)}, u32[]{:S(2)}, u32[]{:S(2)}) %collective-permute-start.1) | collective-permute-done | bytes 524320 | tf_op jit(solution)/shard_map/ppermute | solution.py:155
  16.5 1.4 collective-permute-done.refs_0_
  17.9 0.5 collective-permute-start.6
  18.8 1.7 collective-permute-start.4
  20.6 0.8 copy-done.3
  21.4 1.0 copy-done.4
  22.5 9.3 %shard_map.42.refs_4_ = f32[1024,128]{1,0:T(8,128)S(1)} custom-call(s32[4]{0:T(128)S(1)} %pad_add_fusion.3.ids_ref, bf16[2,1024,16384]{2,1,0:T(8,128)(2,1)} %gram_ref.29, bf16[2,1024,128]{2,1,0:T(8,128)(2,1)S(1)} %collective-permute-done.refs_0_, bf16[2,1024,128]{2,1,0:T(8,128)(2,1)S(1)} %collective-permute-done.1.refs_1_, ...), custom_call_target="tpu_custom_call" | custom-call | flops 2147483648 | bytes 16777216 | tf_op jit(solution)/shard_map/pallas_call | solution.py:113
  31.8 0.5 collective-permute-done.3.refs_0_
  32.4 0.5 collective-permute-start.10
  32.9 1.7 collective-permute-start.7
  35.0 0.8 copy-done.5
  35.8 1.0 copy-done.6
  36.9 9.3 %shard_map.43.refs_4_ = f32[1024,128]{1,0:T(8,128)S(1)} custom-call(s32[4]{0:T(128)S(1)} %pad_add_fusion.5.ids_ref, bf16[2,1024,16384]{2,1,0:T(8,128)(2,1)} %gram_ref.29, bf16[2,1024,128]{2,1,0:T(8,128)(2,1)S(1)} %collective-permute-done.3.refs_0_, bf16[2,1024,128]{2,1,0:T(8,128)(2,1)S(1)} %collective-permute-done.4.refs_1_, ...), custom_call_target="tpu_custom_call" | custom-call | flops 2147483648 | bytes 16777216 | tf_op jit(solution)/shard_map/pallas_call | solution.py:113
  46.2 0.5 collective-permute-done.7.refs_0_
  46.7 1.4 collective-permute-done.8.refs_1_
  48.1 0.5 collective-permute-start.14
  49.1 1.7 collective-permute-start.11
  50.9 9.1 %shard_map.44.refs_2_ = f32[1024,128]{1,0:T(8,128)S(1)} custom-call(s32[4]{0:T(128)S(1)} %pad_add_fusion.7.ids_ref, bf16[2,1024,16384]{2,1,0:T(8,128)(2,1)} %gram_ref.29, bf16[2,1024,128]{2,1,0:T(8,128)(2,1)S(1)} %collective-permute-done.7.refs_0_, bf16[2,1024,128]{2,1,0:T(8,128)(2,1)S(1)} %collective-permute-done.8.refs_1_, ...), custom_call_target="tpu_custom_call" | custom-call | flops 2147483648 | bytes 16777216 | tf_op jit(solution)/shard_map/pallas_call | solution.py:113
  60.4 1.8 collective-permute-done.15.refs_1_
  62.2 5.7 %shard_map.45 = (f32[1024,128]{1,0:T(8,128)S(1)}, f32[1040,128]{1,0:T(8,128)S(1)}) custom-call(s32[2]{0:T(128)S(1)} %pad_add_fusion.ids_ref, bf16[2,1024,16384]{2,1,0:T(8,128)(2,1)} %gram_ref.29, bf16[2,1024,128]{2,1,0:T(8,128)(2,1)S(1)} %constant_dynamic-update-slice_fusion.refs_0_, bf16[2,1024,128]{2,1,0:T(8,128)(2,1)S(1)} %collective-permute-done.15.refs_1_, ...), custom_call_target="tpu_custom_call" | custom-call | flops 1073741824 | bytes 8388608 | tf_op jit(solution)/shard_map/pallas_call | solution.py:113
  68.5 1.7 collective-permute-start.16
  70.3 5.8 %shard_map.46.refs_4_ = f32[1024,128]{1,0:T(8,128)S(1)} custom-call(s32[2]{0:T(128)S(1)} %pad_add_fusion.1.ids_ref, bf16[2,1024,16384]{2,1,0:T(8,128)(2,1)} %gram_ref.29, f32[1024,128]{1,0:T(8,128)S(1)} %get-tuple-element.57.refs_0_, f32[1040,128]{1,0:T(8,128)S(1)} %convert_element_type.97.refs_1_), custom_call_target="tpu_custom_call" | custom-call | flops 2147483648 | bytes 8388608 | tf_op jit(solution)/shard_map/pallas_call | solution.py:113
  76.0 0.8 collective-permute-done.17
  76.9 0.5 collective-permute-start.22
  77.4 1.7 collective-permute-start.19
  79.6 9.6 %shard_map.47.refs_4_ = f32[1024,128]{1,0:T(8,128)S(1)} custom-call(s32[4]{0:T(128)S(1)} %pad_add_fusion.3.ids_ref, bf16[2,1024,16384]{2,1,0:T(8,128)(2,1)} %gram_ref.29, f32[1040,128]{1,0:T(8,128)S(1)} %convert_element_type.98.refs_0_, f32[1040,128]{1,0:T(8,128)S(1)} %convert_element_type.99.refs_1_, f32[1040,128]{1,0:T(8,128)S(1)} %convert_element_type.100.refs_2_, ...), custom_call_target="tpu_custom_call" | custom-call | flops 4294967296 | bytes 16777216 | tf_op jit(solution)/shard_map/pallas_call | solution.py:113
  89.4 0.5 collective-permute-start.26
  89.9 1.7 collective-permute-start.23
  92.1 9.6 %shard_map.48.refs_4_ = f32[1024,128]{1,0:T(8,128)S(1)} custom-call(s32[4]{0:T(128)S(1)} %pad_add_fusion.5.ids_ref, bf16[2,1024,16384]{2,1,0:T(8,128)(2,1)} %gram_ref.29, f32[1040,128]{1,0:T(8,128)S(1)} %convert_element_type.102.refs_0_, f32[1040,128]{1,0:T(8,128)S(1)} %convert_element_type.103.refs_1_, f32[1040,128]{1,0:T(8,128)S(1)} %convert_element_type.104.refs_2_, ...), custom_call_target="tpu_custom_call" | custom-call | flops 4294967296 | bytes 16777216 | tf_op jit(solution)/shard_map/pallas_call | solution.py:113
  101.8 0.5 collective-permute-start.30
  102.5 1.8 collective-permute-start.27
  104.7 9.6 %shard_map.49.refs_2_ = f32[1024,128]{1,0:T(8,128)S(1)} custom-call(s32[4]{0:T(128)S(1)} %pad_add_fusion.7.ids_ref, bf16[2,1024,16384]{2,1,0:T(8,128)(2,1)} %gram_ref.29, f32[1040,128]{1,0:T(8,128)S(1)} %convert_element_type.106.refs_0_, f32[1040,128]{1,0:T(8,128)S(1)} %convert_element_type.107.refs_1_, f32[1040,128]{1,0:T(8,128)S(1)} %convert_element_type.108.refs_2_, ...), custom_call_target="tpu_custom_call" | custom-call | flops 4294967296 | bytes 16777216 | tf_op jit(solution)/shard_map/pallas_call | solution.py:113
  114.5 1.5 collective-permute-done.31
  116.1 6.1 %shard_map.50 = (f32[1024,128]{1,0:T(8,128)S(1)}, f32[1040,128]{1,0:T(8,128)S(1)}) custom-call(s32[2]{0:T(128)S(1)} %pad_add_fusion.ids_ref, bf16[2,1024,16384]{2,1,0:T(8,128)(2,1)} %gram_ref.29, f32[1040,128]{1,0:T(8,128)S(1)} %convert_element_type.110.refs_0_, f32[1040,128]{1,0:T(8,128)S(1)} %convert_element_type.111.refs_1_, ...), custom_call_target="tpu_custom_call" | custom-call | flops 2147483648 | bytes 8388608 | tf_op jit(solution)/shard_map/pallas_call | solution.py:113
  122.4 1.7 collective-permute-start.33
  124.1 0.4 collective-permute-start.32
  124.5 5.8 %shard_map.51.refs_4_ = f32[1024,128]{1,0:T(8,128)S(1)} custom-call(s32[2]{0:T(128)S(1)} %pad_add_fusion.1.ids_ref, bf16[2,1024,16384]{2,1,0:T(8,128)(2,1)} %gram_ref.29, f32[1024,128]{1,0:T(8,128)S(1)} %get-tuple-element.71.refs_0_, f32[1040,128]{1,0:T(8,128)S(1)} %convert_element_type.113.refs_1_), custom_call_target="tpu_custom_call" | custom-call | flops 2147483648 | bytes 8388608 | tf_op jit(solution)/shard_map/pallas_call | solution.py:113
  130.3 0.8 collective-permute-done.33
  131.1 1.4 collective-permute-done.32
  132.5 0.5 collective-permute-start.38
  133.4 1.7 collective-permute-start.36
  135.2 9.6 %shard_map.52.refs_4_ = f32[1024,128]{1,0:T(8,128)S(1)} custom-call(s32[4]{0:T(128)S(1)} %pad_add_fusion.3.ids_ref, bf16[2,1024,16384]{2,1,0:T(8,128)(2,1)} %gram_ref.29, f32[1040,128]{1,0:T(8,128)S(1)} %convert_element_type.114.refs_0_, f32[1040,128]{1,0:T(8,128)S(1)} %convert_element_type.115.refs_1_, f32[1040,128]{1,0:T(8,128)S(1)} %convert_element_type.116.refs_2_, ...), custom_call_target="tpu_custom_call" | custom-call | flops 4294967296 | bytes 16777216 | tf_op jit(solution)/shard_map/pallas_call | solution.py:113
  145.0 0.5 collective-permute-start.42
  145.8 1.7 collective-permute-start.40
  147.7 9.6 %shard_map.53.refs_4_ = f32[1024,128]{1,0:T(8,128)S(1)} custom-call(s32[4]{0:T(128)S(1)} %pad_add_fusion.5.ids_ref, bf16[2,1024,16384]{2,1,0:T(8,128)(2,1)} %gram_ref.29, f32[1040,128]{1,0:T(8,128)S(1)} %convert_element_type.118.refs_0_, f32[1040,128]{1,0:T(8,128)S(1)} %convert_element_type.119.refs_1_, f32[1040,128]{1,0:T(8,128)S(1)} %convert_element_type.120.refs_2_, ...), custom_call_target="tpu_custom_call" | custom-call | flops 4294967296 | bytes 16777216 | tf_op jit(solution)/shard_map/pallas_call | solution.py:113
  157.4 0.5 collective-permute-start.46
  158.1 0.4 collective-permute-start.43
  158.5 1.7 collective-permute-start.44
  160.3 9.6 %shard_map.54.refs_2_ = f32[1024,128]{1,0:T(8,128)S(1)} custom-call(s32[4]{0:T(128)S(1)} %pad_add_fusion.7.ids_ref, bf16[2,1024,16384]{2,1,0:T(8,128)(2,1)} %gram_ref.29, f32[1040,128]{1,0:T(8,128)S(1)} %convert_element_type.122.refs_0_, f32[1040,128]{1,0:T(8,128)S(1)} %convert_element_type.123.refs_1_, f32[1040,128]{1,0:T(8,128)S(1)} %convert_element_type.124.refs_2_, ...), custom_call_target="tpu_custom_call" | custom-call | flops 4294967296 | bytes 16777216 | tf_op jit(solution)/shard_map/pallas_call | solution.py:113
  170.2 1.4 collective-permute-done.47
  171.7 5.9 %shard_map.55 = (f32[1024,128]{1,0:T(8,128)S(1)}, f32[8,128]{1,0:T(8,128)S(1)}) custom-call(s32[2]{0:T(128)S(1)} %pad_add_fusion.ids_ref, bf16[2,1024,16384]{2,1,0:T(8,128)(2,1)} %gram_ref.29, f32[1040,128]{1,0:T(8,128)S(1)} %convert_element_type.126.refs_0_, f32[1040,128]{1,0:T(8,128)S(1)} %convert_element_type.127.refs_1_, ...), custom_call_target="tpu_custom_call" | custom-call | flops 2147483648 | bytes 8388608 | tf_op jit(solution)/shard_map/pallas_call | solution.py:113
  177.6 1.4 collective-permute-start.50
  179.0 0.5 collective-permute-start.49
  179.6 1.2 collective-permute-done.50
  180.7 1.9 collective-permute-done.49
  182.6 1.7 collective-permute-start.51
  184.3 2.0 %collective-permute-done.51 = f32[8,128]{1,0:T(8,128)S(1)} collective-permute-done((f32[8,128]{1,0:T(8,128)S(1)}, f32[8,128]{1,0:T(8,128)S(1)}, u32[]{:S(2)}, u32[]{:S(2)}) %collective-permute-start.51) | collective-permute-done | bytes 4128 | tf_op jit(solution)/shard_map/ppermute | solution.py:155
  186.3 2.6 %collective-permute-start.52 = (f32[8,128]{1,0:T(8,128)S(1)}, f32[8,128]{1,0:T(8,128)S(1)}, u32[]{:S(2)}, u32[]{:S(2)}) collective-permute-start(f32[8,128]{1,0:T(8,128)S(1)} %add.218), channel_id=1, source_target_pairs={{0,8},{1,9},{2,10},{3,11},{4,12},{5,13},{6,14},{7,15},{8,0},{9,1},... | collective-permute-start | bytes 12296 | tf_op jit(solution)/shard_map/ppermute | solution.py:155
  188.9 1.9 collective-permute-done.52
  190.9 1.2 multiply_subtract_fusion
  (130 shorter events, 6.6 us)
Async XLA Ops:
  0.6 3.3 %collective-permute-start.2 = (bf16[2,1024,128]{2,1,0:T(8,128)(2,1)}, bf16[2,1024,128]{2,1,0:T(8,128)(2,1)S(1)}, u32[]{:S(2)}, u32[]{:S(2)}) collective-permute-start(bf16[2,1024,128]{2,1,0:T(8,128)(2,1)} %refs_0_.1), channel_id=1, source_target_pairs={{0,1},{1,0},{2,3},{3,2},{4,5},{5,4},{6,7},{7,6},{8,9},{9,8},{10,11... | collective-permute-start | bytes 1572872 | tf_op jit(solution)/shard_map/ppermute | solution.py:155
  1.1 15.4 %collective-permute-start.1 = (bf16[2,1024,128]{2,1,0:T(8,128)(2,1)}, bf16[2,1024,128]{2,1,0:T(8,128)(2,1)S(1)}, u32[]{:S(2)}, u32[]{:S(2)}) collective-permute-start(bf16[2,1024,128]{2,1,0:T(8,128)(2,1)} %refs_0_.1), channel_id=1, source_target_pairs={{0,2},{1,3},{4,0},{5,1},{8,4},{9,5},{12,8},{13,9},{14,12},{15,13},... | collective-permute-start | bytes 1572872 | tf_op jit(solution)/shard_map/ppermute | solution.py:155
  3.7 14.2 %collective-permute-start = (bf16[2,1024,128]{2,1,0:T(8,128)(2,1)}, bf16[2,1024,128]{2,1,0:T(8,128)(2,1)S(1)}, u32[]{:S(2)}, u32[]{:S(2)}) collective-permute-start(bf16[2,1024,128]{2,1,0:T(8,128)(2,1)} %refs_0_.1), channel_id=1, source_target_pairs={{0,4},{1,5},{4,8},{5,9},{8,12},{9,13},{12,14},{13,15},{14,10},{15,... | collective-permute-start | bytes 1572872 | tf_op jit(solution)/shard_map/ppermute | solution.py:155
  3.9 1.0 copy-start.2
  17.9 2.7 %collective-permute-start.5 = (bf16[2,1024,128]{2,1,0:T(8,128)(2,1)S(1)}, bf16[2,1024,128]{2,1,0:T(8,128)(2,1)S(1)}, u32[]{:S(2)}, u32[]{:S(2)}) collective-permute-start(bf16[2,1024,128]{2,1,0:T(8,128)(2,1)S(1)} %collective-permute-done.refs_0_), channel_id=1, source_target_pairs={{0,1},{1,0},{2,3},{3,2},{4,5},{5,4},{6,7},{7,6},{8,9},{9,8},{10,11... | collective-permute-start | bytes 1572872 | tf_op jit(solution)/shard_map/ppermute | solution.py:155
  17.9 3.5 %collective-permute-start.6 = (bf16[2,1024,128]{2,1,0:T(8,128)(2,1)S(1)}, bf16[2,1024,128]{2,1,0:T(8,128)(2,1)}, u32[]{:S(2)}, u32[]{:S(2)}) collective-permute-start(bf16[2,1024,128]{2,1,0:T(8,128)(2,1)S(1)} %collective-permute-done.1.refs_1_), channel_id=1, source_target_pairs={{0,1},{1,0},{2,3},{3,2},{4,5},{5,4},{6,7},{7,6},{8,9},{9,8},{10,11... | collective-permute-start | bytes 1572872 | tf_op jit(solution)/shard_map/ppermute | solution.py:155
  18.4 13.8 %collective-permute-start.3 = (bf16[2,1024,128]{2,1,0:T(8,128)(2,1)S(1)}, bf16[2,1024,128]{2,1,0:T(8,128)(2,1)S(1)}, u32[]{:S(2)}, u32[]{:S(2)}) collective-permute-start(bf16[2,1024,128]{2,1,0:T(8,128)(2,1)S(1)} %collective-permute-done.refs_0_), channel_id=1, source_target_pairs={{0,4},{1,5},{4,8},{5,9},{8,12},{9,13},{12,14},{13,15},{14,10},{15,... | collective-permute-start | bytes 1572872 | tf_op jit(solution)/shard_map/ppermute | solution.py:155
  18.8 13.6 %collective-permute-start.4 = (bf16[2,1024,128]{2,1,0:T(8,128)(2,1)S(1)}, bf16[2,1024,128]{2,1,0:T(8,128)(2,1)S(1)}, u32[]{:S(2)}, u32[]{:S(2)}) collective-permute-start(bf16[2,1024,128]{2,1,0:T(8,128)(2,1)S(1)} %collective-permute-done.1.refs_1_), channel_id=1, source_target_pairs={{0,2},{1,3},{4,0},{5,1},{8,4},{9,5},{12,8},{13,9},{14,12},{15,13},... | collective-permute-start | bytes 1572872 | tf_op jit(solution)/shard_map/ppermute | solution.py:155
  20.6 0.8 copy-start.3
  21.4 1.0 copy-start.4
  32.3 2.7 %collective-permute-start.9 = (bf16[2,1024,128]{2,1,0:T(8,128)(2,1)S(1)}, bf16[2,1024,128]{2,1,0:T(8,128)(2,1)S(1)}, u32[]{:S(2)}, u32[]{:S(2)}) collective-permute-start(bf16[2,1024,128]{2,1,0:T(8,128)(2,1)S(1)} %collective-permute-done.3.refs_0_), channel_id=1, source_target_pairs={{0,1},{1,0},{2,3},{3,2},{4,5},{5,4},{6,7},{7,6},{8,9},{9,8},{10,11... | collective-permute-start | bytes 1572872 | tf_op jit(solution)/shard_map/ppermute | solution.py:155
  32.4 3.5 %collective-permute-start.10 = (bf16[2,1024,128]{2,1,0:T(8,128)(2,1)S(1)}, bf16[2,1024,128]{2,1,0:T(8,128)(2,1)}, u32[]{:S(2)}, u32[]{:S(2)}) collective-permute-start(bf16[2,1024,128]{2,1,0:T(8,128)(2,1)S(1)} %collective-permute-done.4.refs_1_), channel_id=1, source_target_pairs={{0,1},{1,0},{2,3},{3,2},{4,5},{5,4},{6,7},{7,6},{8,9},{9,8},{10,11... | collective-permute-start | bytes 1572872 | tf_op jit(solution)/shard_map/ppermute | solution.py:155
  32.9 13.8 %collective-permute-start.7 = (bf16[2,1024,128]{2,1,0:T(8,128)(2,1)S(1)}, bf16[2,1024,128]{2,1,0:T(8,128)(2,1)S(1)}, u32[]{:S(2)}, u32[]{:S(2)}) collective-permute-start(bf16[2,1024,128]{2,1,0:T(8,128)(2,1)S(1)} %collective-permute-done.3.refs_0_), channel_id=1, source_target_pairs={{0,4},{1,5},{4,8},{5,9},{8,12},{9,13},{12,14},{13,15},{14,10},{15,... | collective-permute-start | bytes 1572872 | tf_op jit(solution)/shard_map/ppermute | solution.py:155
  34.6 13.6 %collective-permute-start.8 = (bf16[2,1024,128]{2,1,0:T(8,128)(2,1)S(1)}, bf16[2,1024,128]{2,1,0:T(8,128)(2,1)S(1)}, u32[]{:S(2)}, u32[]{:S(2)}) collective-permute-start(bf16[2,1024,128]{2,1,0:T(8,128)(2,1)S(1)} %collective-permute-done.4.refs_1_), channel_id=1, source_target_pairs={{0,2},{1,3},{4,0},{5,1},{8,4},{9,5},{12,8},{13,9},{14,12},{15,13},... | collective-permute-start | bytes 1572872 | tf_op jit(solution)/shard_map/ppermute | solution.py:155
  35.0 0.8 copy-start.5
  35.8 1.0 copy-start.6
  48.1 2.8 %collective-permute-start.13 = (bf16[2,1024,128]{2,1,0:T(8,128)(2,1)S(1)}, bf16[2,1024,128]{2,1,0:T(8,128)(2,1)S(1)}, u32[]{:S(2)}, u32[]{:S(2)}) collective-permute-start(bf16[2,1024,128]{2,1,0:T(8,128)(2,1)S(1)} %collective-permute-done.7.refs_0_), channel_id=1, source_target_pairs={{0,1},{1,0},{2,3},{3,2},{4,5},{5,4},{6,7},{7,6},{8,9},{9,8},{10,11... | collective-permute-start | bytes 1572872 | tf_op jit(solution)/shard_map/ppermute | solution.py:155
  48.1 2.8 %collective-permute-start.14 = (bf16[2,1024,128]{2,1,0:T(8,128)(2,1)S(1)}, bf16[2,1024,128]{2,1,0:T(8,128)(2,1)S(1)}, u32[]{:S(2)}, u32[]{:S(2)}) collective-permute-start(bf16[2,1024,128]{2,1,0:T(8,128)(2,1)S(1)} %collective-permute-done.8.refs_1_), channel_id=1, source_target_pairs={{0,1},{1,0},{2,3},{3,2},{4,5},{5,4},{6,7},{7,6},{8,9},{9,8},{10,11... | collective-permute-start | bytes 1572872 | tf_op jit(solution)/shard_map/ppermute | solution.py:155
  48.8 11.3 %collective-permute-start.12 = (bf16[2,512,128]{2,1,0:T(8,128)(2,1)S(1)}, bf16[2,512,128]{2,1,0:T(8,128)(2,1)S(1)}, u32[]{:S(2)}, u32[]{:S(2)}) collective-permute-start(bf16[2,512,128]{2,1,0:T(8,128)(2,1)S(1)} %slice.31), channel_id=1, source_target_pairs={{0,2},{1,3},{4,0},{5,1},{8,4},{9,5},{12,8},{13,9},{14,12},{15,13},... | collective-permute-start | bytes 786440 | tf_op jit(solution)/shard_map/ppermute | solution.py:155
  49.1 11.0 %collective-permute-start.11 = (bf16[2,512,128]{2,1,0:T(8,128)(2,1)S(1)}, bf16[2,512,128]{2,1,0:T(8,128)(2,1)S(1)}, u32[]{:S(2)}, u32[]{:S(2)}) collective-permute-start(bf16[2,512,128]{2,1,0:T(8,128)(2,1)S(1)} %slice.30), channel_id=1, source_target_pairs={{0,4},{1,5},{4,8},{5,9},{8,12},{9,13},{12,14},{13,15},{14,10},{15,... | collective-permute-start | bytes 786440 | tf_op jit(solution)/shard_map/ppermute | solution.py:155
  60.2 2.0 %collective-permute-start.15 = (bf16[2,1024,128]{2,1,0:T(8,128)(2,1)S(1)}, bf16[2,1024,128]{2,1,0:T(8,128)(2,1)S(1)}, u32[]{:S(2)}, u32[]{:S(2)}) collective-permute-start(bf16[2,1024,128]{2,1,0:T(8,128)(2,1)S(1)} %constant_dynamic-update-slice_fusion.refs_0_), channel_id=1, source_target_pairs={{0,1},{1,0},{2,3},{3,2},{4,5},{5,4},{6,7},{7,6},{8,9},{9,8},{10,11... | collective-permute-start | bytes 1572872 | tf_op jit(solution)/shard_map/ppermute | solution.py:155
  67.9 2.3 %copy-start = (f32[1024,128]{1,0:T(8,128)}, f32[1024,128]{1,0:T(8,128)S(1)}, u32[]{:S(2)}) copy-start(f32[1024,128]{1,0:T(8,128)S(1)} %get-tuple-element.57.refs_0_) | copy-start | bytes 1572868
  68.0 2.2 %collective-permute-start.18 = (f16[1040,128]{1,0:T(8,128)(2,1)S(1)}, f16[1040,128]{1,0:T(8,128)(2,1)S(1)}, u32[]{:S(2)}, u32[]{:S(2)}) collective-permute-start(f16[1040,128]{1,0:T(8,128)(2,1)S(1)} %convert_element_type.96), channel_id=1, source_target_pairs={{0,1},{1,0},{2,3},{3,2},{4,5},{5,4},{6,7},{7,6},{8,9},{9,8},{10,11... | collective-permute-start | bytes 798728 | tf_op jit(solution)/shard_map/ppermute | solution.py:155
  68.2 8.7 %collective-permute-start.17 = (f16[1040,128]{1,0:T(8,128)(2,1)S(1)}, f16[1040,128]{1,0:T(8,128)(2,1)S(1)}, u32[]{:S(2)}, u32[]{:S(2)}) collective-permute-start(f16[1040,128]{1,0:T(8,128)(2,1)S(1)} %convert_element_type.96), channel_id=1, source_target_pairs={{0,2},{1,3},{4,0},{5,1},{8,4},{9,5},{12,8},{13,9},{14,12},{15,13},... | collective-permute-start | bytes 798728 | tf_op jit(solution)/shard_map/ppermute | solution.py:155
  68.5 8.4 %collective-permute-start.16 = (f16[1040,128]{1,0:T(8,128)(2,1)S(1)}, f16[1040,128]{1,0:T(8,128)(2,1)S(1)}, u32[]{:S(2)}, u32[]{:S(2)}) collective-permute-start(f16[1040,128]{1,0:T(8,128)(2,1)S(1)} %convert_element_type.96), channel_id=1, source_target_pairs={{0,4},{1,5},{4,8},{5,9},{8,12},{9,13},{12,14},{13,15},{14,10},{15,... | collective-permute-start | bytes 798728 | tf_op jit(solution)/shard_map/ppermute | solution.py:155
  76.9 2.6 %collective-permute-start.21 = (f16[1040,128]{1,0:T(8,128)(2,1)S(1)}, f16[1040,128]{1,0:T(8,128)(2,1)S(1)}, u32[]{:S(2)}, u32[]{:S(2)}) collective-permute-start(f16[1040,128]{1,0:T(8,128)(2,1)S(1)} %collective-permute-done.16), channel_id=1, source_target_pairs={{0,1},{1,0},{2,3},{3,2},{4,5},{5,4},{6,7},{7,6},{8,9},{9,8},{10,11... | collective-permute-start | bytes 798728 | tf_op jit(solution)/shard_map/ppermute | solution.py:155
  76.9 2.7 %collective-permute-start.22 = (f16[1040,128]{1,0:T(8,128)(2,1)S(1)}, f16[1040,128]{1,0:T(8,128)(2,1)S(1)}, u32[]{:S(2)}, u32[]{:S(2)}) collective-permute-start(f16[1040,128]{1,0:T(8,128)(2,1)S(1)} %collective-permute-done.17), channel_id=1, source_target_pairs={{0,1},{1,0},{2,3},{3,2},{4,5},{5,4},{6,7},{7,6},{8,9},{9,8},{10,11... | collective-permute-start | bytes 798728 | tf_op jit(solution)/shard_map/ppermute | solution.py:155
  77.4 11.9 %collective-permute-start.19 = (f16[1040,128]{1,0:T(8,128)(2,1)S(1)}, f16[1040,128]{1,0:T(8,128)(2,1)S(1)}, u32[]{:S(2)}, u32[]{:S(2)}) collective-permute-start(f16[1040,128]{1,0:T(8,128)(2,1)S(1)} %collective-permute-done.16), channel_id=1, source_target_pairs={{0,4},{1,5},{4,8},{5,9},{8,12},{9,13},{12,14},{13,15},{14,10},{15,... | collective-permute-start | bytes 798728 | tf_op jit(solution)/shard_map/ppermute | solution.py:155
  79.1 10.2 %collective-permute-start.20 = (f16[1040,128]{1,0:T(8,128)(2,1)S(1)}, f16[1040,128]{1,0:T(8,128)(2,1)S(1)}, u32[]{:S(2)}, u32[]{:S(2)}) collective-permute-start(f16[1040,128]{1,0:T(8,128)(2,1)S(1)} %collective-permute-done.17), channel_id=1, source_target_pairs={{0,2},{1,3},{4,0},{5,1},{8,4},{9,5},{12,8},{13,9},{14,12},{15,13},... | collective-permute-start | bytes 798728 | tf_op jit(solution)/shard_map/ppermute | solution.py:155
  89.3 2.7 %collective-permute-start.25 = (f16[1040,128]{1,0:T(8,128)(2,1)S(1)}, f16[1040,128]{1,0:T(8,128)(2,1)S(1)}, u32[]{:S(2)}, u32[]{:S(2)}) collective-permute-start(f16[1040,128]{1,0:T(8,128)(2,1)S(1)} %collective-permute-done.19), channel_id=1, source_target_pairs={{0,1},{1,0},{2,3},{3,2},{4,5},{5,4},{6,7},{7,6},{8,9},{9,8},{10,11... | collective-permute-start | bytes 798728 | tf_op jit(solution)/shard_map/ppermute | solution.py:155
  89.4 2.7 %collective-permute-start.26 = (f16[1040,128]{1,0:T(8,128)(2,1)S(1)}, f16[1040,128]{1,0:T(8,128)(2,1)S(1)}, u32[]{:S(2)}, u32[]{:S(2)}) collective-permute-start(f16[1040,128]{1,0:T(8,128)(2,1)S(1)} %collective-permute-done.20), channel_id=1, source_target_pairs={{0,1},{1,0},{2,3},{3,2},{4,5},{5,4},{6,7},{7,6},{8,9},{9,8},{10,11... | collective-permute-start | bytes 798728 | tf_op jit(solution)/shard_map/ppermute | solution.py:155
  89.9 11.9 %collective-permute-start.23 = (f16[1040,128]{1,0:T(8,128)(2,1)S(1)}, f16[1040,128]{1,0:T(8,128)(2,1)S(1)}, u32[]{:S(2)}, u32[]{:S(2)}) collective-permute-start(f16[1040,128]{1,0:T(8,128)(2,1)S(1)} %collective-permute-done.19), channel_id=1, source_target_pairs={{0,4},{1,5},{4,8},{5,9},{8,12},{9,13},{12,14},{13,15},{14,10},{15,... | collective-permute-start | bytes 798728 | tf_op jit(solution)/shard_map/ppermute | solution.py:155
  91.6 10.2 %collective-permute-start.24 = (f16[1040,128]{1,0:T(8,128)(2,1)S(1)}, f16[1040,128]{1,0:T(8,128)(2,1)S(1)}, u32[]{:S(2)}, u32[]{:S(2)}) collective-permute-start(f16[1040,128]{1,0:T(8,128)(2,1)S(1)} %collective-permute-done.20), channel_id=1, source_target_pairs={{0,2},{1,3},{4,0},{5,1},{8,4},{9,5},{12,8},{13,9},{14,12},{15,13},... | collective-permute-start | bytes 798728 | tf_op jit(solution)/shard_map/ppermute | solution.py:155
  101.7 2.8 %collective-permute-start.29 = (f16[1040,128]{1,0:T(8,128)(2,1)S(1)}, f16[1040,128]{1,0:T(8,128)(2,1)S(1)}, u32[]{:S(2)}, u32[]{:S(2)}) collective-permute-start(f16[1040,128]{1,0:T(8,128)(2,1)S(1)} %collective-permute-done.23), channel_id=1, source_target_pairs={{0,1},{1,0},{2,3},{3,2},{4,5},{5,4},{6,7},{7,6},{8,9},{9,8},{10,11... | collective-permute-start | bytes 798728 | tf_op jit(solution)/shard_map/ppermute | solution.py:155
  101.8 2.8 %collective-permute-start.30 = (f16[1040,128]{1,0:T(8,128)(2,1)S(1)}, f16[1040,128]{1,0:T(8,128)(2,1)S(1)}, u32[]{:S(2)}, u32[]{:S(2)}) collective-permute-start(f16[1040,128]{1,0:T(8,128)(2,1)S(1)} %collective-permute-done.24), channel_id=1, source_target_pairs={{0,1},{1,0},{2,3},{3,2},{4,5},{5,4},{6,7},{7,6},{8,9},{9,8},{10,11... | collective-permute-start | bytes 798728 | tf_op jit(solution)/shard_map/ppermute | solution.py:155
  102.5 11.8 %collective-permute-start.27 = (f16[512,128]{1,0:T(8,128)(2,1)S(1)}, f16[512,128]{1,0:T(8,128)(2,1)S(1)}, u32[]{:S(2)}, u32[]{:S(2)}) collective-permute-start(f16[512,128]{1,0:T(8,128)(2,1)S(1)} %slice.32), channel_id=1, source_target_pairs={{0,4},{1,5},{4,8},{5,9},{8,12},{9,13},{12,14},{13,15},{14,10},{15,... | collective-permute-start | bytes 393224 | tf_op jit(solution)/shard_map/ppermute | solution.py:155
  104.3 10.1 %collective-permute-start.28 = (f16[528,128]{1,0:T(8,128)(2,1)S(1)}, f16[528,128]{1,0:T(8,128)(2,1)S(1)}, u32[]{:S(2)}, u32[]{:S(2)}) collective-permute-start(f16[528,128]{1,0:T(8,128)(2,1)S(1)} %slice.33), channel_id=1, source_target_pairs={{0,2},{1,3},{4,0},{5,1},{8,4},{9,5},{12,8},{13,9},{14,12},{15,13},... | collective-permute-start | bytes 405512 | tf_op jit(solution)/shard_map/ppermute | solution.py:155
  114.4 1.6 collective-permute-start.31
  122.2 2.2 %collective-permute-start.34 = (f16[1040,128]{1,0:T(8,128)(2,1)S(1)}, f16[1040,128]{1,0:T(8,128)(2,1)S(1)}, u32[]{:S(2)}, u32[]{:S(2)}) collective-permute-start(f16[1040,128]{1,0:T(8,128)(2,1)S(1)} %convert_element_type.112), channel_id=1, source_target_pairs={{0,1},{1,0},{2,3},{3,2},{4,5},{5,4},{6,7},{7,6},{8,9},{9,8},{10,11... | collective-permute-start | bytes 798728 | tf_op jit(solution)/shard_map/ppermute | solution.py:155
  122.4 8.7 %collective-permute-start.33 = (f16[1040,128]{1,0:T(8,128)(2,1)S(1)}, f16[1040,128]{1,0:T(8,128)(2,1)S(1)}, u32[]{:S(2)}, u32[]{:S(2)}) collective-permute-start(f16[1040,128]{1,0:T(8,128)(2,1)S(1)} %convert_element_type.112), channel_id=1, source_target_pairs={{0,2},{1,3},{4,0},{5,1},{8,4},{9,5},{12,8},{13,9},{14,12},{15,13},... | collective-permute-start | bytes 798728 | tf_op jit(solution)/shard_map/ppermute | solution.py:155
  124.1 8.4 %collective-permute-start.32 = (f16[1040,128]{1,0:T(8,128)(2,1)S(1)}, f16[1040,128]{1,0:T(8,128)(2,1)S(1)}, u32[]{:S(2)}, u32[]{:S(2)}) collective-permute-start(f16[1040,128]{1,0:T(8,128)(2,1)S(1)} %convert_element_type.112), channel_id=1, source_target_pairs={{0,4},{1,5},{4,8},{5,9},{8,12},{9,13},{12,14},{13,15},{14,10},{15,... | collective-permute-start | bytes 798728 | tf_op jit(solution)/shard_map/ppermute | solution.py:155
  132.5 2.6 %collective-permute-start.37 = (f16[1040,128]{1,0:T(8,128)(2,1)S(1)}, f16[1040,128]{1,0:T(8,128)(2,1)S(1)}, u32[]{:S(2)}, u32[]{:S(2)}) collective-permute-start(f16[1040,128]{1,0:T(8,128)(2,1)S(1)} %collective-permute-done.32), channel_id=1, source_target_pairs={{0,1},{1,0},{2,3},{3,2},{4,5},{5,4},{6,7},{7,6},{8,9},{9,8},{10,11... | collective-permute-start | bytes 798728 | tf_op jit(solution)/shard_map/ppermute | solution.py:155
  132.5 2.7 %collective-permute-start.38 = (f16[1040,128]{1,0:T(8,128)(2,1)S(1)}, f16[1040,128]{1,0:T(8,128)(2,1)S(1)}, u32[]{:S(2)}, u32[]{:S(2)}) collective-permute-start(f16[1040,128]{1,0:T(8,128)(2,1)S(1)} %collective-permute-done.33), channel_id=1, source_target_pairs={{0,1},{1,0},{2,3},{3,2},{4,5},{5,4},{6,7},{7,6},{8,9},{9,8},{10,11... | collective-permute-start | bytes 798728 | tf_op jit(solution)/shard_map/ppermute | solution.py:155
  133.0 11.9 %collective-permute-start.35 = (f16[1040,128]{1,0:T(8,128)(2,1)S(1)}, f16[1040,128]{1,0:T(8,128)(2,1)S(1)}, u32[]{:S(2)}, u32[]{:S(2)}) collective-permute-start(f16[1040,128]{1,0:T(8,128)(2,1)S(1)} %collective-permute-done.32), channel_id=1, source_target_pairs={{0,4},{1,5},{4,8},{5,9},{8,12},{9,13},{12,14},{13,15},{14,10},{15,... | collective-permute-start | bytes 798728 | tf_op jit(solution)/shard_map/ppermute | solution.py:155
  133.4 11.5 %collective-permute-start.36 = (f16[1040,128]{1,0:T(8,128)(2,1)S(1)}, f16[1040,128]{1,0:T(8,128)(2,1)S(1)}, u32[]{:S(2)}, u32[]{:S(2)}) collective-permute-start(f16[1040,128]{1,0:T(8,128)(2,1)S(1)} %collective-permute-done.33), channel_id=1, source_target_pairs={{0,2},{1,3},{4,0},{5,1},{8,4},{9,5},{12,8},{13,9},{14,12},{15,13},... | collective-permute-start | bytes 798728 | tf_op jit(solution)/shard_map/ppermute | solution.py:155
  144.9 2.7 %collective-permute-start.41 = (f16[1040,128]{1,0:T(8,128)(2,1)S(1)}, f16[1040,128]{1,0:T(8,128)(2,1)S(1)}, u32[]{:S(2)}, u32[]{:S(2)}) collective-permute-start(f16[1040,128]{1,0:T(8,128)(2,1)S(1)} %collective-permute-done.35), channel_id=1, source_target_pairs={{0,1},{1,0},{2,3},{3,2},{4,5},{5,4},{6,7},{7,6},{8,9},{9,8},{10,11... | collective-permute-start | bytes 798728 | tf_op jit(solution)/shard_map/ppermute | solution.py:155
  145.0 2.7 %collective-permute-start.42 = (f16[1040,128]{1,0:T(8,128)(2,1)S(1)}, f16[1040,128]{1,0:T(8,128)(2,1)S(1)}, u32[]{:S(2)}, u32[]{:S(2)}) collective-permute-start(f16[1040,128]{1,0:T(8,128)(2,1)S(1)} %collective-permute-done.36), channel_id=1, source_target_pairs={{0,1},{1,0},{2,3},{3,2},{4,5},{5,4},{6,7},{7,6},{8,9},{9,8},{10,11... | collective-permute-start | bytes 798728 | tf_op jit(solution)/shard_map/ppermute | solution.py:155
  145.5 11.9 %collective-permute-start.39 = (f16[1040,128]{1,0:T(8,128)(2,1)S(1)}, f16[1040,128]{1,0:T(8,128)(2,1)S(1)}, u32[]{:S(2)}, u32[]{:S(2)}) collective-permute-start(f16[1040,128]{1,0:T(8,128)(2,1)S(1)} %collective-permute-done.35), channel_id=1, source_target_pairs={{0,4},{1,5},{4,8},{5,9},{8,12},{9,13},{12,14},{13,15},{14,10},{15,... | collective-permute-start | bytes 798728 | tf_op jit(solution)/shard_map/ppermute | solution.py:155
  145.8 11.5 %collective-permute-start.40 = (f16[1040,128]{1,0:T(8,128)(2,1)S(1)}, f16[1040,128]{1,0:T(8,128)(2,1)S(1)}, u32[]{:S(2)}, u32[]{:S(2)}) collective-permute-start(f16[1040,128]{1,0:T(8,128)(2,1)S(1)} %collective-permute-done.36), channel_id=1, source_target_pairs={{0,2},{1,3},{4,0},{5,1},{8,4},{9,5},{12,8},{13,9},{14,12},{15,13},... | collective-permute-start | bytes 798728 | tf_op jit(solution)/shard_map/ppermute | solution.py:155
  147.7 22.4 %copy-start.1 = (f32[1024,128]{1,0:T(8,128)S(1)}, f32[1024,128]{1,0:T(8,128)}, u32[]{:S(2)}) copy-start(f32[1024,128]{1,0:T(8,128)} %copy-done) | copy-start | bytes 1572868
  157.4 2.8 %collective-permute-start.45 = (f16[1040,128]{1,0:T(8,128)(2,1)S(1)}, f16[1040,128]{1,0:T(8,128)(2,1)S(1)}, u32[]{:S(2)}, u32[]{:S(2)}) collective-permute-start(f16[1040,128]{1,0:T(8,128)(2,1)S(1)} %collective-permute-done.39), channel_id=1, source_target_pairs={{0,1},{1,0},{2,3},{3,2},{4,5},{5,4},{6,7},{7,6},{8,9},{9,8},{10,11... | collective-permute-start | bytes 798728 | tf_op jit(solution)/shard_map/ppermute | solution.py:155
  157.4 2.8 %collective-permute-start.46 = (f16[1040,128]{1,0:T(8,128)(2,1)S(1)}, f16[1040,128]{1,0:T(8,128)(2,1)S(1)}, u32[]{:S(2)}, u32[]{:S(2)}) collective-permute-start(f16[1040,128]{1,0:T(8,128)(2,1)S(1)} %collective-permute-done.40), channel_id=1, source_target_pairs={{0,1},{1,0},{2,3},{3,2},{4,5},{5,4},{6,7},{7,6},{8,9},{9,8},{10,11... | collective-permute-start | bytes 798728 | tf_op jit(solution)/shard_map/ppermute | solution.py:155
  158.1 11.8 %collective-permute-start.43 = (f16[512,128]{1,0:T(8,128)(2,1)S(1)}, f16[512,128]{1,0:T(8,128)(2,1)S(1)}, u32[]{:S(2)}, u32[]{:S(2)}) collective-permute-start(f16[512,128]{1,0:T(8,128)(2,1)S(1)} %slice.34), channel_id=1, source_target_pairs={{0,4},{1,5},{4,8},{5,9},{8,12},{9,13},{12,14},{13,15},{14,10},{15,... | collective-permute-start | bytes 393224 | tf_op jit(solution)/shard_map/ppermute | solution.py:155
  158.5 11.4 %collective-permute-start.44 = (f16[528,128]{1,0:T(8,128)(2,1)S(1)}, f16[528,128]{1,0:T(8,128)(2,1)S(1)}, u32[]{:S(2)}, u32[]{:S(2)}) collective-permute-start(f16[528,128]{1,0:T(8,128)(2,1)S(1)} %slice.35), channel_id=1, source_target_pairs={{0,2},{1,3},{4,0},{5,1},{8,4},{9,5},{12,8},{13,9},{14,12},{15,13},... | collective-permute-start | bytes 405512 | tf_op jit(solution)/shard_map/ppermute | solution.py:155
  170.0 1.6 collective-permute-start.47
  177.6 3.1 %collective-permute-start.50 = (f32[8,128]{1,0:T(8,128)S(1)}, f32[8,128]{1,0:T(8,128)S(1)}, u32[]{:S(2)}, u32[]{:S(2)}) collective-permute-start(f32[8,128]{1,0:T(8,128)S(1)} %get-tuple-element.84), channel_id=1, source_target_pairs={{0,3},{1,2},{2,1},{3,0},{4,7},{5,6},{6,5},{7,4},{8,11},{9,10},{10,... | collective-permute-start | bytes 12296 | tf_op jit(solution)/shard_map/ppermute | solution.py:155
  179.0 3.6 %collective-permute-start.49 = (f32[8,128]{1,0:T(8,128)S(1)}, f32[8,128]{1,0:T(8,128)S(1)}, u32[]{:S(2)}, u32[]{:S(2)}) collective-permute-start(f32[8,128]{1,0:T(8,128)S(1)} %get-tuple-element.84), channel_id=1, source_target_pairs={{0,2},{1,3},{2,0},{3,1},{4,6},{5,7},{6,4},{7,5},{8,10},{9,11},{10,... | collective-permute-start | bytes 12296 | tf_op jit(solution)/shard_map/ppermute | solution.py:155
  179.5 3.2 %collective-permute-start.48 = (f32[8,128]{1,0:T(8,128)S(1)}, f32[8,128]{1,0:T(8,128)S(1)}, u32[]{:S(2)}, u32[]{:S(2)}) collective-permute-start(f32[8,128]{1,0:T(8,128)S(1)} %get-tuple-element.84), channel_id=1, source_target_pairs={{0,1},{1,0},{2,3},{3,2},{4,5},{5,4},{6,7},{7,6},{8,9},{9,8},{10,11... | collective-permute-start | bytes 12296 | tf_op jit(solution)/shard_map/ppermute | solution.py:155
  182.6 3.7 %collective-permute-start.51 = (f32[8,128]{1,0:T(8,128)S(1)}, f32[8,128]{1,0:T(8,128)S(1)}, u32[]{:S(2)}, u32[]{:S(2)}) collective-permute-start(f32[8,128]{1,0:T(8,128)S(1)} %add_add_fusion), channel_id=1, source_target_pairs={{0,4},{1,5},{2,6},{3,7},{4,0},{5,1},{6,2},{7,3},{8,12},{9,13},{10,... | collective-permute-start | bytes 12296 | tf_op jit(solution)/shard_map/ppermute | solution.py:155
  186.3 4.5 %collective-permute-start.52 = (f32[8,128]{1,0:T(8,128)S(1)}, f32[8,128]{1,0:T(8,128)S(1)}, u32[]{:S(2)}, u32[]{:S(2)}) collective-permute-start(f32[8,128]{1,0:T(8,128)S(1)} %add.218), channel_id=1, source_target_pairs={{0,8},{1,9},{2,10},{3,11},{4,12},{5,13},{6,14},{7,15},{8,0},{9,1},... | collective-permute-start | bytes 12296 | tf_op jit(solution)/shard_map/ppermute | solution.py:155
